TPU v7x, 32 devices: a whole 2x2x4 slice. The times are simulated.
32 devices in a mesh: seq: 8 (over z, x), head: 4 (over y, core).
Axes of the slice: x: 2, y: 2, z: 4, core: 2. Of those that a mesh axis runs over, the one named last changes fastest.
Arguments:
- queries: bfloat16 [4096, 4096], P(('seq', 'head')), may hold values from -100 to 100
- keys: bfloat16 [4096, 4096], P(('seq', 'head')), may hold values from -6 to 6
- values: bfloat16 [4096, 4096], P(('seq', 'head')), may hold values from -6 to 6
- doc_blocks: int32 [8], replicated, may hold values from 1 to 16, 32 in all
Outputs:
- attended: bfloat16 [4096, 4096], P(('seq', 'head'))
Inputs may be any that keep to these rules, and one draw needn't show every extreme that they name: `doc_blocks`: the 8 lengths sum to 32; the longest is 16.
All inputs are finite; a program needn't handle non-finite values.
Results may differ from a plain program's by a relative error of at most 0.0031.
Values may be sent and summed in bfloat16 or wider, within the bound.
A program may use at most 64 MiB of HBM per device.

v0:
```python
import jax
import jax.numpy as jnp
from jax import lax
from jax.sharding import PartitionSpec as P

H = 32
DH = 128
BLOCK = 128


def carried_in(value, axis, join, neutral):
    count, mine = (lax.axis_size(axis), lax.axis_index(axis))
    pieces = jax.tree.map(lambda part: lax.all_gather(part, axis), value)
    total = jax.tree.map(
        lambda part, zero: jnp.full_like(part, 0) + jnp.asarray(zero, part.dtype), value, neutral
    )

    def step(position, total):
        longer = join(total, jax.tree.map(lambda part: part[position], pieces))
        return jax.tree.map(lambda new, old: jnp.where(position < mine, new, old), longer, total)

    return lax.fori_loop(0, count - 1, step, total)


def doc_index(positions, doc_blocks):
    doc_ends = jnp.cumsum(doc_blocks) * BLOCK
    return jnp.sum((positions[:, None] >= doc_ends[None, :-1]).astype(jnp.int32), axis=1)


def softmax_part(query_rows, key_rows, value_rows, doc_here):
    stretch_len = query_rows.shape[0]
    row_block = min(512, stretch_len)
    inv_root = DH ** (-0.5)
    key_pos = jnp.arange(stretch_len, dtype=jnp.int32)

    def score_block(index):
        first = index * row_block
        query_block = lax.dynamic_slice_in_dim(query_rows, first, row_block, 0)
        doc_block = lax.dynamic_slice_in_dim(doc_here, first, row_block, 0)
        query_pos = first + jnp.arange(row_block, dtype=jnp.int32)
        scores = (
            jnp.einsum("qhd,khd->hqk", query_block, key_rows, preferred_element_type=jnp.float32)
            * inv_root
        )
        allowed = (key_pos[None, :] <= query_pos[:, None]) & (
            doc_here[None, :] == doc_block[:, None]
        )
        scores = jnp.where(allowed[None], scores, -1e30)
        peak = jnp.max(scores, axis=-1, keepdims=True)
        expo = jnp.exp(scores - peak)
        weights = (expo / jnp.sum(expo, axis=-1, keepdims=True)).astype(jnp.bfloat16)
        return jnp.einsum("hqk,khd->qhd", weights, value_rows, preferred_element_type=jnp.float32)

    blocks = lax.map(score_block, jnp.arange(stretch_len // row_block, dtype=jnp.int32))
    return blocks.reshape(stretch_len, query_rows.shape[1], DH)


def head_work(query_rows, key_rows, value_rows, doc_blocks):
    stretch_len = query_rows.shape[0]
    stretch_pos = lax.axis_index("seq")
    stretch_base = stretch_pos * stretch_len
    positions = stretch_base + jnp.arange(stretch_len, dtype=jnp.int32)
    doc_here = doc_index(positions, doc_blocks)
    first_doc = doc_here[0]
    last_doc = doc_here[-1]
    tail_keys = key_rows * (doc_here == last_doc).astype(key_rows.dtype)[:, None, None]
    increment = jnp.einsum(
        "lhd,lhe->hde", tail_keys, value_rows, preferred_element_type=jnp.float32
    )
    zero_state = jnp.zeros_like(increment)
    doc_starts = (jnp.cumsum(doc_blocks) - doc_blocks) * BLOCK
    starts_here = jnp.any(
        (doc_starts >= stretch_base) & (doc_starts < stretch_base + stretch_len)
    ).astype(jnp.float32)

    def combine(earlier, later):
        summed = jnp.where(later[1] > 0.0, later[0], earlier[0] + later[0])
        return (summed, jnp.maximum(earlier[1], later[1]))

    prefix, unused = carried_in(
        (increment, starts_here), "seq", combine, (zero_state, jnp.float32(0.0))
    )
    earlier_doc = doc_index(jnp.maximum(stretch_base - 1, 0)[None], doc_blocks)[0]
    carried = (doc_here == first_doc) & (stretch_pos > 0) & (earlier_doc == first_doc)
    linear = jnp.einsum(
        "lhd,hde->lhe", query_rows.astype(jnp.float32), prefix, precision=lax.Precision.HIGHEST
    )
    normed = linear * lax.rsqrt(jnp.mean(linear * linear, axis=-1, keepdims=True) + 1e-06)
    normed = normed * carried.astype(jnp.float32)[:, None, None]
    soft = softmax_part(query_rows, key_rows, value_rows, doc_here)
    return (soft + normed).astype(jnp.bfloat16)


def on_device(queries, keys, values, doc_blocks):
    tokens_here = queries.shape[0]
    query_three = queries.reshape(tokens_here, H, DH)
    key_three = keys.reshape(tokens_here, H, DH)
    value_three = values.reshape(tokens_here, H, DH)
    query_rows, key_rows, value_rows = (
        lax.all_to_all(query_three, "head", split_axis=1, concat_axis=0, tiled=True),
        lax.all_to_all(key_three, "head", split_axis=1, concat_axis=0, tiled=True),
        lax.all_to_all(value_three, "head", split_axis=1, concat_axis=0, tiled=True),
    )
    mixed = head_work(query_rows, key_rows, value_rows, doc_blocks)
    result = lax.all_to_all(mixed, "head", split_axis=0, concat_axis=1, tiled=True)
    return result.reshape(tokens_here, H * DH)


def solution(mesh):
    placed = (P(("seq", "head"), None), P(("seq", "head"), None), P(("seq", "head"), None), P())
    return jax.shard_map(
        on_device, mesh=mesh, in_specs=placed, out_specs=P(("seq", "head"), None), check_vma=False
    )
```

profile of v0, /device:TPU:0, one launch (start us, length us, event | category | flops | bytes accessed | tf_op | source)
XLA Modules:
  0.0 173.2 jit_solution(12139564033923638693)
XLA Ops:
  6.5 0.0 copy-start.2
  6.5 0.0 copy-start.1
  6.5 1.7 copy.52
  8.2 1.3 copy.53
  9.6 4.2 %all-to-all-start.1 = ((bf16[128,32,128]{2,0,1:T(8,128)(2,1)}), bf16[128,32,128]{2,0,1:T(8,128)(2,1)S(1)}, u32[]{:S(2)}, u32[]{:S(2)}) async-start(bf16[128,32,128]{2,0,1:T(8,128)(2,1)} %copy.53), calls=%async_computation.1 | async-start | bytes 2097152 | tf_op jit(solution)/shard_map/all_to_all | solution.py:101
  13.8 0.0 copy-done.2
  13.8 0.2 reduce-window.9
  14.0 0.0 copy-done.1
  14.0 0.7 copy.56
  14.7 1.3 copy.57
  16.0 12.3 %all-to-all-done.1 = bf16[128,32,128]{2,0,1:T(8,128)(2,1)S(1)} async-done(((bf16[128,32,128]{2,0,1:T(8,128)(2,1)}), bf16[128,32,128]{2,0,1:T(8,128)(2,1)S(1)}, u32[]{:S(2)}, u32[]{:S(2)}) %all-to-all-start.1) | async-done | bytes 1048608 | tf_op jit(solution)/shard_map/all_to_all | solution.py:101
  28.3 3.5 %all-to-all-start.2 = ((bf16[128,32,128]{2,0,1:T(8,128)(2,1)}), bf16[128,32,128]{2,0,1:T(8,128)(2,1)S(1)}, u32[]{:S(2)}, u32[]{:S(2)}) async-start(bf16[128,32,128]{2,0,1:T(8,128)(2,1)} %copy.57), calls=%async_computation.2 | async-start | bytes 2097152 | tf_op jit(solution)/shard_map/all_to_all | solution.py:102
  31.8 0.0 all-gather.3.cloned.1.call-start
  31.9 0.7 fusion.17
  32.6 0.1 convert_reduce_fusion
  32.7 0.6 fusion.21
  34.5 1.2 and_convert_fusion
  35.7 0.1 copy.55
  35.8 10.4 %all-to-all-done.2 = bf16[128,32,128]{2,0,1:T(8,128)(2,1)S(1)} async-done(((bf16[128,32,128]{2,0,1:T(8,128)(2,1)}), bf16[128,32,128]{2,0,1:T(8,128)(2,1)S(1)}, u32[]{:S(2)}, u32[]{:S(2)}) %all-to-all-start.2) | async-done | bytes 1048608 | tf_op jit(solution)/shard_map/all_to_all | solution.py:102
  46.2 0.1 copy.59
  46.3 0.0 copy-start.3
  46.4 1.4 fusion.11
  47.8 0.0 all-gather.3.cloned.1.call-update
  47.8 1.6 copy.48
  49.4 1.3 copy.49
  50.7 4.2 %all-to-all-start = ((bf16[128,32,128]{2,0,1:T(8,128)(2,1)}), bf16[128,32,128]{2,0,1:T(8,128)(2,1)}, u32[]{:S(2)}, u32[]{:S(2)}) async-start(bf16[128,32,128]{2,0,1:T(8,128)(2,1)} %copy.49), calls=%async_computation | async-start | bytes 2097152 | tf_op jit(solution)/shard_map/all_to_all | solution.py:100
  55.0 0.6 and_reduce_fusion
  56.2 0.0 copy-done.3
  56.2 0.6 dynamic-slice
  56.8 0.7 dynamic-update-slice
  57.5 22.6 %all-reduce = f32[8]{0:T(128)S(1)} all-reduce(f32[8]{0:T(128)S(1)} %dynamic-update-slice), channel_id=1, replica_groups=mesh['seq'=8,'head'=4] {'seq'}, use_global_device_ids=true, to_apply=%add | all-reduce | flops 8 | bytes 64
  80.1 0.2 fusion.13
  80.3 0.0 all-to-all-done
  80.3 2.3 %copy.51 = bf16[4,128,8,128]{3,1,0,2:T(8,128)(2,1)} copy(bf16[4,128,8,128]{3,1,2,0:T(8,128)(2,1)} %bitcast.5) | data formatting | bytes 2097152 | tf_op jit(solution)/shard_map/all_to_all | solution.py:100
  82.6 7.7 %fusion.22 = (f32[8,512]{1,0:T(8,128)S(1)}, f32[8,512,512]{1,2,0:T(8,128)}) fusion(pred[512,512]{0,1:T(8,128)(4,1)S(1)} %fusion.13, bf16[512,8,128]{2,0,1:T(8,128)(2,1)} %bitcast.68, bf16[512,8,128]{2,0,1:T(8,128)(2,1)S(1)} %bitcast.67), kind=kOutput, calls=%fused_computation.38 | convolution fusion | flops 545260032 | bytes 10764288 | tf_op jit(solution)/shard_map/while/body/eval_jaxpr/sub | solution.py:50
  90.3 0.0 copy-start
  90.3 32.3 %all-gather.3.cloned.1.call-done = f32[64,128,128]{2,1,0:T(8,128)} async-done(((f32[8,128,128]{2,1,0:T(8,128)}), f32[64,128,128]{2,1,0:T(8,128)}) %all-gather.3.cloned.1.call-update) | async-done | bytes 4194320 | tf_op jit(solution)/shard_map/all_gather | solution.py:13
  122.7 17.8 %while.18 = (s32[]{:T(128)}, f32[8,128,128]{2,1,0:T(8,128)S(1)}, s32[]{:T(128)}, f32[8]{0:T(128)S(1)}, f32[8,8,128,128]{3,2,1,0:T(8,128)}, /*index=5*/s32[]{:T(128)}, s32[]{:T(128)}, f32[1]{0:T(128)}) while((s32[]{:T(128)}, f32[8,128,128]{2,1,0:T(8,128)S(1)}, s32[]{:T(128)}, f32[8]{0:T(128)S(1)}, f32[8,8,128,128]{3,2,1,0:T(8,128)}, ...), condition=%wide.region_6.7_spmd.clone, body=%wide.region_5.6_spmd.clone.sunk | while | flops 524293 | bytes 1573003 | solution.py:22
  122.7 0.6 dynamic_slice.27
  123.9 1.3 fusion.32
  125.2 0.6 dynamic_slice.27
  126.4 1.3 fusion.32
  127.8 0.6 dynamic_slice.27
  129.0 1.3 fusion.32
  130.3 0.6 dynamic_slice.27
  131.5 1.3 fusion.32
  132.9 0.6 dynamic_slice.27
  134.1 1.3 fusion.32
  135.4 0.6 dynamic_slice.27
  136.6 1.3 fusion.32
  138.0 0.6 dynamic_slice.27
  139.2 1.3 fusion.32
  140.5 0.0 copy-done
  140.5 1.3 fusion.7
  141.9 5.2 %fusion.10 = bf16[512,8,128]{2,0,1:T(8,128)(2,1)S(1)} fusion(f32[8,128,512]{1,2,0:T(8,128)S(1)} %get-tuple-element.158, bf16[512,8,128]{2,0,1:T(8,128)(2,1)S(1)} %bitcast.65, f32[8,512,512]{1,2,0:T(8,128)} %get-tuple-element.156, f32[8,512]{1,0:T(8,128)S(1)} %get-tuple-element.155, f32[512]{0:T(512)S(1)} %get-tuple-element.149, f32[512,8]{0,1:T(8,128)S(1)} %add_rsqrt_fusion), kind=kOutput, calls=%fused_computation.16 | convolution fusion | flops 543162368 | bytes 12617728 | tf_op jit(solution)/shard_map/while/body/eval_jaxpr/hqk,khd->qhd/dot_general | solution.py:52
  147.1 0.7 copy.64
  147.8 17.0 %all_to_all.69 = bf16[512,8,128]{2,1,0:T(8,128)(2,1)S(1)} all-to-all(bf16[512,8,128]{2,1,0:T(8,128)(2,1)S(1)} %copy.64), channel_id=1, replica_groups=mesh['seq'=8,'head'=4] {'head'}, dimensions={0} | all-to-all | bytes 2097152 | tf_op jit(solution)/shard_map/all_to_all | solution.py:105
  164.8 0.2 copy.65
  165.0 1.4 copy.75
  (5 shorter events, 0.0 us)
Async XLA Ops:
  6.5 7.3 %copy-start.2 = (s32[8]{0:T(128)S(1)}, s32[8]{0:T(128)}, u32[]{:S(2)}) copy-start(s32[8]{0:T(128)} %param.9) | copy-start | bytes 100
  6.5 7.5 %copy-start.1 = (bf16[128,4096]{1,0:T(8,128)(2,1)S(1)}, bf16[128,4096]{1,0:T(8,128)(2,1)}, u32[]{:S(2)}) copy-start(bf16[128,4096]{1,0:T(8,128)(2,1)} %param.8) | copy-start | bytes 3145732
  9.6 18.7 %all-to-all-start.1 = ((bf16[128,32,128]{2,0,1:T(8,128)(2,1)}), bf16[128,32,128]{2,0,1:T(8,128)(2,1)S(1)}, u32[]{:S(2)}, u32[]{:S(2)}) async-start(bf16[128,32,128]{2,0,1:T(8,128)(2,1)} %copy.53), calls=%async_computation.1 | async-start | bytes 2097152 | tf_op jit(solution)/shard_map/all_to_all | solution.py:101
  28.3 18.0 %all-to-all-start.2 = ((bf16[128,32,128]{2,0,1:T(8,128)(2,1)}), bf16[128,32,128]{2,0,1:T(8,128)(2,1)S(1)}, u32[]{:S(2)}, u32[]{:S(2)}) async-start(bf16[128,32,128]{2,0,1:T(8,128)(2,1)} %copy.57), calls=%async_computation.2 | async-start | bytes 2097152 | tf_op jit(solution)/shard_map/all_to_all | solution.py:102
  31.8 90.9 %all-gather.3.cloned.1.call-start = ((), (), s32[]{:S(2)}) async-start(), calls=%async_computation.4 | async-start | bytes 4718592 | tf_op jit(solution)/shard_map/all_gather | solution.py:13
  46.3 9.9 %copy-start.3 = (u32[32]{0:T(128)S(1)}, u32[32]{0:T(128)}, u32[]{:S(2)}) copy-start(u32[32]{0:T(128)} %constant.86) | copy-start | bytes 388
  50.7 29.6 %all-to-all-start = ((bf16[128,32,128]{2,0,1:T(8,128)(2,1)}), bf16[128,32,128]{2,0,1:T(8,128)(2,1)}, u32[]{:S(2)}, u32[]{:S(2)}) async-start(bf16[128,32,128]{2,0,1:T(8,128)(2,1)} %copy.49), calls=%async_computation | async-start | bytes 2097152 | tf_op jit(solution)/shard_map/all_to_all | solution.py:100
  90.3 50.2 %copy-start = (bf16[4,128,8,128]{3,1,0,2:T(8,128)(2,1)S(1)}, bf16[4,128,8,128]{3,1,0,2:T(8,128)(2,1)}, u32[]{:S(2)}) copy-start(bf16[4,128,8,128]{3,1,0,2:T(8,128)(2,1)} %copy.51) | copy-start | bytes 3145732
Sparse Core Ops, SparseCore 0:
  47.9 74.7 all-gather.2
where the time goes:
time: 174 us; the launch traced here: 173 us
  waiting for transfers between devices  55 us (32%)
  blocking collectives  39.6 us (23%)
  local copies, waits for them, and re-layouts  18.9 us (11%)
  matrix products  15.7 us (9%)
  between operations  15.4 us (9%)
  other arithmetic  12.1 us (7%)
  starting transfers between devices  12 us (7%)
  loops' own time  4.43 us (3%)
    all_gather x1, waiting for transfers between devices, carried_in(): pieces = jax.tree.map(lambda part: lax.all_gather(part, axis), value)  32.3 us
    unnamed x1, blocking collectives  22.6 us
    all_to_all x1, blocking collectives, on_device(): lax.all_to_all(mixed, 'head', split_axis=0, concat_axis=1, tiled=True)  17 us
    all_to_all x1, waiting for transfers between devices, on_device(): lax.all_to_all(key_three, 'head', split_axis=1, concat_axis=0, tiled=True)  12.3 us
    all_to_all x1, waiting for transfers between devices, on_device(): lax.all_to_all(value_three, 'head', split_axis=1, concat_axis=0, tiled=True)  10.4 us
    select_n x7, other arithmetic, step(): jnp.where(position < mine, new, old)  9.09 us
    sub x1, matrix products, score_block(): expo = jnp.exp(scores - peak)  7.72 us
    unnamed x15, local copies, waits for them, and re-layouts  6.66 us
  transfers between devices with their start and end apart: 4, of which 3 were waited for; matrix products, arithmetic and copies ran while one was open for 12% of the time, Pallas kernels for 0%

commit v1 on v0

v1 whole, which is shorter than its diff:
```python
import functools

import jax
import jax.numpy as jnp
from jax import lax
from jax.experimental import pallas as pl
from jax.experimental.pallas import tpu as pltpu
from jax.sharding import PartitionSpec as P

H = 32
DH = 128
BLOCK = 128
NDOC = 8
MESH = pl.DeviceIdType.MESH
F32 = jnp.float32
BF16 = jnp.bfloat16


def kernel(n_seq, n_head, tokens, q_hbm, k_hbm, v_hbm, doc_ref, out_hbm,
           q_buf, k_buf, v_buf, o_buf, inc, pair_in, chain_in, chain_out, prefix,
           in_send, in_recv, in_local, pair_send, pair_recv, chain_send, chain_recv,
           out_send, out_recv, out_local):
    heads = H // n_head
    span = n_head * tokens
    chunks = min(4, heads)
    per = heads // chunks
    width = per * DH
    outer = n_seq // 2
    seq, me = lax.axis_index("seq"), lax.axis_index("head")
    z, x = seq // 2, seq % 2
    partner = 2 * z + (1 - x)

    barrier = pltpu.get_barrier_semaphore()

    def greet(to_seq, to_head):
        pl.semaphore_signal(barrier, inc=1, device_id=(to_seq, to_head), device_id_type=MESH)

    for r in range(1, n_head):
        greet(seq, (me + r) % n_head)
    greet(partner, me)

    greet((seq + 2) % n_seq, me)
    greet((seq + n_seq - 2) % n_seq, me)
    pl.semaphore_wait(barrier, n_head + 2)

    mine = pl.ds(pl.multiple_of(me * tokens, tokens), tokens)
    arrays = ((k_hbm, k_buf), (v_hbm, v_buf), (q_hbm, q_buf))

    def columns(owner, chunk):
        return pl.ds(pl.multiple_of(owner * (heads * DH) + chunk * width, DH), width)

    def incoming(a, chunk, r):
        source, target = arrays[a]
        to = (me + r) % n_head
        here = pl.ds(chunk * width, width)
        if r == 0:
            return pltpu.make_async_copy(
                source.at[:, columns(me, chunk)], target.at[mine, here], in_local.at[a, chunk])
        return pltpu.make_async_remote_copy(
            src_ref=source.at[:, columns(to, chunk)], dst_ref=target.at[mine, here],
            send_sem=in_send.at[a, chunk, r], recv_sem=in_recv.at[a, chunk, r],
            device_id=(seq, to), device_id_type=MESH)

    def send_in(a, chunk):
        for r in (2, 3, 1, 0) if n_head == 4 else range(n_head):
            incoming(a, chunk, r).start()

    def wait_in(a, chunk):
        for r in range(n_head):
            copy = incoming(a, chunk, r)
            copy.wait() if r == 0 else copy.wait_recv()

    for chunk in range(chunks):
        send_in(0, chunk)
        send_in(1, chunk)
    for chunk in range(chunks):
        send_in(2, chunk)

    ends, total = [], 0
    for d in range(NDOC - 1):
        total = total + doc_ref[d]
        ends.append(total * BLOCK)

    def doc_of(position):
        found = jnp.zeros_like(position)
        for end in ends:
            found = found + jnp.where(position >= end, 1, 0).astype(jnp.int32)
        return found

    def same(one, other):
        return jnp.where(one == other, 1.0, 0.0).astype(F32)

    base = seq * span
    pair_base = 2 * z * span
    before = doc_of(pair_base - 1)
    first0, last0 = doc_of(pair_base), doc_of(pair_base + span - 1)
    first1, last1 = doc_of(pair_base + span), doc_of(pair_base + 2 * span - 1)
    first_here, last_here = doc_of(base), doc_of(base + span - 1)
    keep_pair = same(last0, last1)
    keep_chain = same(before, last0)
    is_second = jnp.where(x == 1, 1.0, 0.0).astype(F32)
    use_chain = (1.0 - is_second) * same(before, first0) + is_second * same(last0, first1) * keep_chain
    use_pair = is_second * same(last0, first1)

    doc_rows = doc_of(base + lax.broadcasted_iota(jnp.int32, (span, DH), 0))
    tail = doc_rows == last_here
    carried = jnp.where(doc_rows == first_here, 1.0, 0.0).astype(F32)
    doc_cols = doc_of(base + lax.broadcasted_iota(jnp.int32, (1, span), 1))

    def head_columns(head):
        return pl.ds(pl.multiple_of(head * DH, DH), DH)

    def increment(chunk):
        wait_in(0, chunk)
        wait_in(1, chunk)
        for head in range(chunk * per, (chunk + 1) * per):
            keys = k_buf[:, head * DH:(head + 1) * DH]
            keys = jnp.where(tail, keys.astype(F32), 0.0).astype(BF16)
            inc[head] = lax.dot_general(
                keys, v_buf[:, head * DH:(head + 1) * DH], (((0,), (0,)), ((), ())),
                preferred_element_type=F32)

    def some(chunk):
        return pl.ds(chunk * per, per)

    def pair_copy(chunk):
        return pltpu.make_async_remote_copy(
            src_ref=inc.at[some(chunk)], dst_ref=pair_in.at[some(chunk)],
            send_sem=pair_send.at[chunk], recv_sem=pair_recv.at[chunk],
            device_id=(partner, me), device_id_type=MESH)

    def chain_copy(chunk, to):
        return pltpu.make_async_remote_copy(
            src_ref=chain_out.at[some(chunk)], dst_ref=chain_in.at[some(chunk)],
            send_sem=chain_send.at[chunk], recv_sem=chain_recv.at[chunk],
            device_id=(to, me), device_id_type=MESH)

    def forward(chunk):
        pair_copy(chunk).wait_recv()

        @pl.when(z > 0)
        def _():
            chain_copy(chunk, seq - 2).wait_recv()

        @pl.when(z == 0)
        def _():
            chain_in[some(chunk)] = jnp.zeros((per, DH, DH), F32)

        first_inc = is_second * pair_in[some(chunk)] + (1.0 - is_second) * inc[some(chunk)]
        second_inc = is_second * inc[some(chunk)] + (1.0 - is_second) * pair_in[some(chunk)]
        chain = chain_in[some(chunk)]

        @pl.when(z < outer - 1)
        def _():
            chain_out[some(chunk)] = second_inc + keep_pair * (first_inc + keep_chain * chain)
            chain_copy(chunk, seq + 2).start()

        prefix[some(chunk)] = use_pair * first_inc + use_chain * chain

    scale = 1.4426950408889634 * DH ** (-0.5)

    def soft_rows(head, i, start):
        rows = pl.ds(start, BLOCK)
        count = (i + 1) * tokens
        queries = q_buf[rows, head_columns(head)]
        scores = lax.dot_general(
            queries, k_buf[:count, head_columns(head)], (((1,), (1,)), ((), ())),
            preferred_element_type=F32)
        row = start + lax.broadcasted_iota(jnp.int32, (BLOCK, 1), 0)
        doc_here = doc_of(base + row)
        allowed = doc_here == doc_cols[:, :count]
        allowed = allowed & (lax.broadcasted_iota(jnp.int32, (1, count), 1) <= row)
        scores = jnp.where(allowed, scores, -1e30)
        peak = jnp.max(scores, axis=-1, keepdims=True)
        expo = jnp.exp2((scores - peak) * scale)
        norm = 1.0 / jnp.sum(expo, axis=-1, keepdims=True)
        weights = (expo * norm).astype(BF16)
        return jnp.dot(weights, v_buf[:count, head_columns(head)], preferred_element_type=F32)

    def linear_rows(head, start):
        rows = pl.ds(start, BLOCK)
        queries = q_buf[rows, head_columns(head)]
        state = prefix[head]
        high = state.astype(BF16)
        rest = state - high.astype(F32)
        mid = rest.astype(BF16)
        low = (rest - mid.astype(F32)).astype(BF16)
        linear = jnp.dot(queries, high, preferred_element_type=F32) + (
            jnp.dot(queries, mid, preferred_element_type=F32)
            + jnp.dot(queries, low, preferred_element_type=F32))
        normed = linear * lax.rsqrt(jnp.mean(linear * linear, axis=-1, keepdims=True) + 1e-06)
        here = doc_of(base + start + lax.broadcasted_iota(jnp.int32, (BLOCK, DH), 0))
        return normed * jnp.where(here == first_here, 1.0, 0.0).astype(F32)

    def attend(chunk):
        @pl.loop(chunk * per, (chunk + 1) * per)
        def _(head):
            for i in range(n_head):
                def block(start):
                    result = soft_rows(head, i, start) + linear_rows(head, start)
                    o_buf[pl.ds(start, BLOCK), head_columns(head)] = result.astype(BF16)

                if tokens == BLOCK:
                    block(i * tokens)
                else:
                    @pl.loop(0, tokens // BLOCK)
                    def _(r):
                        block(pl.multiple_of(i * tokens + r * BLOCK, BLOCK))

    def outgoing(chunk, r):
        to = (me + r) % n_head
        source = o_buf.at[pl.ds(pl.multiple_of(to * tokens, tokens), tokens), pl.ds(chunk * width, width)]
        target = out_hbm.at[:, columns(me, chunk)]
        if r == 0:
            return pltpu.make_async_copy(source, target, out_local.at[chunk])
        return pltpu.make_async_remote_copy(
            src_ref=source, dst_ref=target,
            send_sem=out_send.at[chunk, r], recv_sem=out_recv.at[chunk, r],
            device_id=(seq, to), device_id_type=MESH)

    for chunk in range(chunks):
        increment(chunk)
        pair_copy(chunk).start()
        if chunk > 0:
            forward(chunk - 1)
    forward(chunks - 1)
    for chunk in range(chunks):
        wait_in(2, chunk)
        attend(chunk)
        for r in (2, 3, 1, 0) if n_head == 4 else range(n_head):
            outgoing(chunk, r).start()

    for chunk in range(chunks):
        for a in range(3):
            for r in range(1, n_head):
                incoming(a, chunk, r).wait_send()
        pair_copy(chunk).wait_send()

        @pl.when(z < outer - 1)
        def _():
            chain_copy(chunk, seq + 2).wait_send()

        outgoing(chunk, 0).wait()
        for r in range(1, n_head):
            outgoing(chunk, r).wait()


def on_device(n_seq, n_head, queries, keys, values, doc_blocks):
    tokens, width = queries.shape
    heads = H // n_head
    span = tokens * n_head
    chunks = min(4, heads)
    states = pltpu.VMEM((heads, DH, DH), F32)
    rows = pltpu.VMEM((span, heads * DH), BF16)
    dma = pltpu.SemaphoreType.DMA
    anywhere = pl.BlockSpec(memory_space=pl.ANY)
    return pl.pallas_call(
        functools.partial(kernel, n_seq, n_head, tokens),
        out_shape=jax.ShapeDtypeStruct((tokens, width), BF16),
        in_specs=[anywhere] * 3 + [pl.BlockSpec(memory_space=pltpu.SMEM)],
        out_specs=anywhere,
        scratch_shapes=[
            rows, rows, rows, rows, states, states, states, states, states,
            dma((3, chunks, n_head)), dma((3, chunks, n_head)), dma((3, chunks)),
            dma((chunks,)), dma((chunks,)), dma((chunks,)), dma((chunks,)),
            dma((chunks, n_head)), dma((chunks, n_head)), dma((chunks,)),
        ],
        compiler_params=pltpu.CompilerParams(
            collective_id=0, has_side_effects=True, vmem_limit_bytes=56 * 1024 * 1024),
        cost_estimate=pl.CostEstimate(
            flops=4 * span * span * heads * DH, bytes_accessed=8 * tokens * width,
            transcendentals=span * span * heads),
    )(queries, keys, values, doc_blocks)


def solution(mesh):
    n_seq, n_head = mesh.shape["seq"], mesh.shape["head"]
    placed = (P(("seq", "head"), None),) * 3 + (P(),)
    return jax.shard_map(
        functools.partial(on_device, n_seq, n_head),
        mesh=mesh, in_specs=placed, out_specs=P(("seq", "head"), None), check_vma=False,
    )
```

time: 174 us -> 66.7 us (0.38)
  the two profiles are of different devices: /device:TPU:0 before, /device:TPU:29 now
where the time goes in v1:
time: 66.7 us; the launch traced here: 66.5 us
  Pallas kernels  64.2 us (96%)
  local copies, waits for them, and re-layouts  2.29 us (3%)
    pallas_call x1, Pallas kernels, on_device(): pl.pallas_call(functools.partial(kernel, n_seq, n_head, tokens), out_shap...  64.2 us
    unnamed x1, local copies, waits for them, and re-layouts  2.29 us

profile of v1, /device:TPU:29, one launch (start us, length us, event | category | flops | bytes accessed | tf_op | source)
XLA Modules:
  0.0 66.5 jit_solution(16778861221037791499)
XLA Ops:
  0.0 64.2 %shard_map.46 = bf16[128,4096]{1,0:T(8,128)(2,1)} custom-call(bf16[128,4096]{1,0:T(8,128)(2,1)} %q_hbm.1, bf16[128,4096]{1,0:T(8,128)(2,1)} %k_hbm.1, bf16[128,4096]{1,0:T(8,128)(2,1)} %v_hbm.1, s32[8]{0:T(128)} %doc_ref.1), custom_call_target="tpu_custom_call" | custom-call | flops 1073741824 | bytes 4194304 | tf_op jit(solution)/shard_map/pallas_call | solution.py:257
  64.3 2.3 %copy.6 = bf16[128,4096]{1,0:T(8,128)(2,1)} copy(bf16[128,4096]{1,0:T(8,128)(2,1)} %shard_map.46) | data formatting | bytes 2097152

commit v2 on v1

--- a/solution.py
+++ b/solution.py
@@ -17,7 +17,7 @@
 
 
 def kernel(n_seq, n_head, tokens, q_hbm, k_hbm, v_hbm, doc_ref, out_hbm,
-           q_buf, k_buf, v_buf, o_buf, inc, pair_in, chain_in, chain_out, prefix,
+           q_buf, k_buf, v_buf, o_buf, inc, pair_in, chain_in, chain_out, prefix, bias, carried, soft,
            in_send, in_recv, in_local, pair_send, pair_recv, chain_send, chain_recv,
            out_send, out_recv, out_local):
     heads = H // n_head
@@ -70,10 +70,13 @@
             copy = incoming(a, chunk, r)
             copy.wait() if r == 0 else copy.wait_recv()
 
+    early = max(chunks - 2, 0)
     for chunk in range(chunks):
         send_in(0, chunk)
         send_in(1, chunk)
-    for chunk in range(chunks):
+        if chunk == early:
+            send_in(2, 0)
+    for chunk in range(1, chunks):
         send_in(2, chunk)
 
     ends, total = [], 0
@@ -104,8 +107,14 @@
 
     doc_rows = doc_of(base + lax.broadcasted_iota(jnp.int32, (span, DH), 0))
     tail = doc_rows == last_here
-    carried = jnp.where(doc_rows == first_here, 1.0, 0.0).astype(F32)
+    carried[...] = jnp.where(doc_rows == first_here, 1.0, 0.0).astype(F32)
     doc_cols = doc_of(base + lax.broadcasted_iota(jnp.int32, (1, span), 1))
+    for i in range(n_head):
+        start, count = i * tokens, (i + 1) * tokens
+        row = start + lax.broadcasted_iota(jnp.int32, (tokens, 1), 0)
+        allowed = doc_of(base + row) == doc_cols[:, :count]
+        allowed = allowed & (lax.broadcasted_iota(jnp.int32, (1, count), 1) <= row)
+        bias[start:start + tokens, :count] = jnp.where(allowed, 0.0, -1e30).astype(F32)
 
     def head_columns(head):
         return pl.ds(pl.multiple_of(head * DH, DH), DH)
@@ -155,80 +164,86 @@
             chain_out[some(chunk)] = second_inc + keep_pair * (first_inc + keep_chain * chain)
             chain_copy(chunk, seq + 2).start()
 
-        prefix[some(chunk)] = use_pair * first_inc + use_chain * chain
-
-    scale = 1.4426950408889634 * DH ** (-0.5)
-
-    def soft_rows(head, i, start):
-        rows = pl.ds(start, BLOCK)
-        count = (i + 1) * tokens
-        queries = q_buf[rows, head_columns(head)]
-        scores = lax.dot_general(
-            queries, k_buf[:count, head_columns(head)], (((1,), (1,)), ((), ())),
-            preferred_element_type=F32)
-        row = start + lax.broadcasted_iota(jnp.int32, (BLOCK, 1), 0)
-        doc_here = doc_of(base + row)
-        allowed = doc_here == doc_cols[:, :count]
-        allowed = allowed & (lax.broadcasted_iota(jnp.int32, (1, count), 1) <= row)
-        scores = jnp.where(allowed, scores, -1e30)
-        peak = jnp.max(scores, axis=-1, keepdims=True)
-        expo = jnp.exp2((scores - peak) * scale)
-        norm = 1.0 / jnp.sum(expo, axis=-1, keepdims=True)
-        weights = (expo * norm).astype(BF16)
-        return jnp.dot(weights, v_buf[:count, head_columns(head)], preferred_element_type=F32)
-
-    def linear_rows(head, start):
-        rows = pl.ds(start, BLOCK)
-        queries = q_buf[rows, head_columns(head)]
-        state = prefix[head]
+        state = use_pair * first_inc + use_chain * chain
         high = state.astype(BF16)
         rest = state - high.astype(F32)
         mid = rest.astype(BF16)
-        low = (rest - mid.astype(F32)).astype(BF16)
-        linear = jnp.dot(queries, high, preferred_element_type=F32) + (
-            jnp.dot(queries, mid, preferred_element_type=F32)
-            + jnp.dot(queries, low, preferred_element_type=F32))
-        normed = linear * lax.rsqrt(jnp.mean(linear * linear, axis=-1, keepdims=True) + 1e-06)
-        here = doc_of(base + start + lax.broadcasted_iota(jnp.int32, (BLOCK, DH), 0))
-        return normed * jnp.where(here == first_here, 1.0, 0.0).astype(F32)
-
-    def attend(chunk):
+        prefix[0, some(chunk)] = high
+        prefix[1, some(chunk)] = mid
+        prefix[2, some(chunk)] = (rest - mid.astype(F32)).astype(BF16)
+
+    scale = 1.4426950408889634 * DH ** (-0.5)
+
+    def soft_part(chunk):
+        wait_in(2, chunk)
+
         @pl.loop(chunk * per, (chunk + 1) * per)
         def _(head):
+            here = head_columns(head)
             for i in range(n_head):
-                def block(start):
-                    result = soft_rows(head, i, start) + linear_rows(head, start)
-                    o_buf[pl.ds(start, BLOCK), head_columns(head)] = result.astype(BF16)
-
-                if tokens == BLOCK:
-                    block(i * tokens)
-                else:
-                    @pl.loop(0, tokens // BLOCK)
-                    def _(r):
-                        block(pl.multiple_of(i * tokens + r * BLOCK, BLOCK))
-
-    def outgoing(chunk, r):
+                start, count = i * tokens, (i + 1) * tokens
+                scores = lax.dot_general(
+                    q_buf[start:count, here], k_buf[:count, here], (((1,), (1,)), ((), ())),
+                    preferred_element_type=F32)
+                scores = scores + bias[start:count, :count]
+                peak = jnp.max(scores, axis=-1, keepdims=True)
+                expo = jnp.exp2((scores - peak) * scale)
+                norm = 1.0 / jnp.sum(expo, axis=-1, keepdims=True)
+                soft[start:count, head_columns(head - chunk * per)] = jnp.dot(
+                    (expo * norm).astype(BF16), v_buf[:count, here], preferred_element_type=F32)
+
+    def linear_part(chunk):
+        @pl.loop(chunk * per, (chunk + 1) * per)
+        def _(head):
+            here = head_columns(head)
+            queries = q_buf[:, here]
+            linear = jnp.dot(queries, prefix[0, head], preferred_element_type=F32) + (
+                jnp.dot(queries, prefix[1, head], preferred_element_type=F32)
+                + jnp.dot(queries, prefix[2, head], preferred_element_type=F32))
+            normed = linear * lax.rsqrt(jnp.mean(linear * linear, axis=-1, keepdims=True) + 1e-06)
+            result = soft[:, head_columns(head - chunk * per)] + normed * carried[...]
+            o_buf[:, here] = result.astype(BF16)
+            for r in (2, 3, 1, 0) if n_head == 4 else range(n_head):
+                outgoing(head, r).start()
+
+    def outgoing(head, r):
         to = (me + r) % n_head
-        source = o_buf.at[pl.ds(pl.multiple_of(to * tokens, tokens), tokens), pl.ds(chunk * width, width)]
-        target = out_hbm.at[:, columns(me, chunk)]
+        source = o_buf.at[pl.ds(pl.multiple_of(to * tokens, tokens), tokens), head_columns(head)]
+        target = out_hbm.at[:, head_columns(me * heads + head)]
         if r == 0:
-            return pltpu.make_async_copy(source, target, out_local.at[chunk])
+            return pltpu.make_async_copy(source, target, out_local.at[head])
         return pltpu.make_async_remote_copy(
             src_ref=source, dst_ref=target,
-            send_sem=out_send.at[chunk, r], recv_sem=out_recv.at[chunk, r],
+            send_sem=out_send.at[head, r], recv_sem=out_recv.at[head, r],
             device_id=(seq, to), device_id_type=MESH)
 
-    for chunk in range(chunks):
+    last = chunks - 1
+    for chunk in range(last):
         increment(chunk)
         pair_copy(chunk).start()
         if chunk > 0:
             forward(chunk - 1)
-    forward(chunks - 1)
-    for chunk in range(chunks):
-        wait_in(2, chunk)
-        attend(chunk)
-        for r in (2, 3, 1, 0) if n_head == 4 else range(n_head):
-            outgoing(chunk, r).start()
+    if last > 1:
+        soft_part(0)
+        linear_part(0)
+    increment(last)
+    pair_copy(last).start()
+    if last > 0:
+        forward(last - 1)
+    begin = 1 if last > 1 else 0
+    for chunk in range(begin, chunks):
+        if chunk < last:
+            @pl.when(z == chunk - begin)
+            def _():
+                forward(last)
+
+        soft_part(chunk)
+        if chunk == last:
+            @pl.when(z >= last - begin)
+            def _():
+                forward(last)
+
+        linear_part(chunk)
 
     for chunk in range(chunks):
         for a in range(3):
@@ -240,9 +255,10 @@
         def _():
             chain_copy(chunk, seq + 2).wait_send()
 
-        outgoing(chunk, 0).wait()
-        for r in range(1, n_head):
-            outgoing(chunk, r).wait()
+    @pl.loop(0, heads)
+    def _(head):
+        for r in range(n_head):
+            outgoing(head, r).wait()
 
 
 def on_device(n_seq, n_head, queries, keys, values, doc_blocks):
@@ -260,10 +276,12 @@
         in_specs=[anywhere] * 3 + [pl.BlockSpec(memory_space=pltpu.SMEM)],
         out_specs=anywhere,
         scratch_shapes=[
-            rows, rows, rows, rows, states, states, states, states, states,
+            rows, rows, rows, rows, states, states, states, states,
+            pltpu.VMEM((3, heads, DH, DH), BF16), pltpu.VMEM((span, span), F32),
+            pltpu.VMEM((span, DH), F32), pltpu.VMEM((span, heads // chunks * DH), F32),
             dma((3, chunks, n_head)), dma((3, chunks, n_head)), dma((3, chunks)),
             dma((chunks,)), dma((chunks,)), dma((chunks,)), dma((chunks,)),
-            dma((chunks, n_head)), dma((chunks, n_head)), dma((chunks,)),
+            dma((heads, n_head)), dma((heads, n_head)), dma((heads,)),
         ],
         compiler_params=pltpu.CompilerParams(
             collective_id=0, has_side_effects=True, vmem_limit_bytes=56 * 1024 * 1024),

time: 66.7 us -> 64.5 us (0.967)
  Pallas kernels: 64.2 us -> 61.9 us
    pallas_call x1, Pallas kernels: 64.2 us -> 61.9 us  [on_device(): pl.pallas_call(functools.partial(kernel, n_seq, n_head, tokens), out_shap...]
where the time goes in v2:
time: 64.5 us; the launch traced here: 64.1 us
  Pallas kernels  61.9 us (96%)
  local copies, waits for them, and re-layouts  2.29 us (4%)
    pallas_call x1, Pallas kernels, on_device(): pl.pallas_call(functools.partial(kernel, n_seq, n_head, tokens), out_shap...  61.9 us
    unnamed x1, local copies, waits for them, and re-layouts  2.29 us

profile of v2, /device:TPU:29, one launch (start us, length us, event | category | flops | bytes accessed | tf_op | source)
XLA Modules:
  0.0 64.1 jit_solution(2989537065755822033)
XLA Ops:
  0.0 61.9 %shard_map.46 = bf16[128,4096]{1,0:T(8,128)(2,1)} custom-call(bf16[128,4096]{1,0:T(8,128)(2,1)} %q_hbm.1, bf16[128,4096]{1,0:T(8,128)(2,1)} %k_hbm.1, bf16[128,4096]{1,0:T(8,128)(2,1)} %v_hbm.1, s32[8]{0:T(128)} %doc_ref.1), custom_call_target="tpu_custom_call" | custom-call | flops 1073741824 | bytes 4194304 | tf_op jit(solution)/shard_map/pallas_call | solution.py:273
  61.9 2.3 %copy.6 = bf16[128,4096]{1,0:T(8,128)(2,1)} copy(bf16[128,4096]{1,0:T(8,128)(2,1)} %shard_map.46) | data formatting | bytes 2097152

commit v3 on v2

--- a/solution.py
+++ b/solution.py
@@ -70,14 +70,24 @@
             copy = incoming(a, chunk, r)
             copy.wait() if r == 0 else copy.wait_recv()
 
-    early = max(chunks - 2, 0)
-    for chunk in range(chunks):
-        send_in(0, chunk)
-        send_in(1, chunk)
-        if chunk == early:
-            send_in(2, 0)
-    for chunk in range(1, chunks):
-        send_in(2, chunk)
+    groups = [("kv", chunk) for chunk in range(chunks)]
+    groups.insert(max(chunks - 1, 2), ("q", 0))
+    groups += [("q", chunk) for chunk in range(1, chunks)]
+
+    def send_group(index):
+        if index < len(groups):
+            kind, chunk = groups[index]
+            for a in (0, 1) if kind == "kv" else (2,):
+                send_in(a, chunk)
+
+    def wait_group(index):
+        kind, chunk = groups[index]
+        for a in (0, 1) if kind == "kv" else (2,):
+            wait_in(a, chunk)
+        send_group(index + 2)
+
+    send_group(0)
+    send_group(1)
 
     ends, total = [], 0
     for d in range(NDOC - 1):
@@ -120,8 +130,6 @@
         return pl.ds(pl.multiple_of(head * DH, DH), DH)
 
     def increment(chunk):
-        wait_in(0, chunk)
-        wait_in(1, chunk)
         for head in range(chunk * per, (chunk + 1) * per):
             keys = k_buf[:, head * DH:(head + 1) * DH]
             keys = jnp.where(tail, keys.astype(F32), 0.0).astype(BF16)
@@ -175,8 +183,6 @@
     scale = 1.4426950408889634 * DH ** (-0.5)
 
     def soft_part(chunk):
-        wait_in(2, chunk)
-
         @pl.loop(chunk * per, (chunk + 1) * per)
         def _(head):
             here = head_columns(head)
@@ -217,33 +223,29 @@
             send_sem=out_send.at[head, r], recv_sem=out_recv.at[head, r],
             device_id=(seq, to), device_id_type=MESH)
 
-    last = chunks - 1
-    for chunk in range(last):
-        increment(chunk)
-        pair_copy(chunk).start()
-        if chunk > 0:
-            forward(chunk - 1)
-    if last > 1:
-        soft_part(0)
-        linear_part(0)
-    increment(last)
-    pair_copy(last).start()
-    if last > 0:
-        forward(last - 1)
-    begin = 1 if last > 1 else 0
-    for chunk in range(begin, chunks):
-        if chunk < last:
-            @pl.when(z == chunk - begin)
-            def _():
-                forward(last)
-
-        soft_part(chunk)
-        if chunk == last:
-            @pl.when(z >= last - begin)
-            def _():
-                forward(last)
-
-        linear_part(chunk)
+    ready = [groups.index(("kv", chunk)) + 1 for chunk in range(chunks)]
+    final = [min(groups.index(("q", chunk + 1)) - 1 if chunk + 1 < chunks else len(groups) - 1, ready[chunk] + 3)
+             for chunk in range(chunks)]
+    for chunk in range(chunks):
+        final[chunk] = max(final[chunk], groups.index(("q", chunk)))
+    for index, (kind, chunk) in enumerate(groups):
+        wait_group(index)
+        if kind == "kv":
+            increment(chunk)
+            pair_copy(chunk).start()
+        else:
+            soft_part(chunk)
+        for other in range(chunks):
+            if ready[other] <= index <= final[other]:
+                turn = index - ready[other]
+
+                @pl.when(z >= turn if index == final[other] else z == turn)
+                def _():
+                    forward(other)
+
+        for other in range(chunks):
+            if final[other] == index:
+                linear_part(other)
 
     for chunk in range(chunks):
         for a in range(3):

time: 64.5 us -> 57.3 us (0.89)
  Pallas kernels: 61.9 us -> 54.8 us
    pallas_call x1, Pallas kernels: 61.9 us -> 54.8 us  [on_device(): pl.pallas_call(functools.partial(kernel, n_seq, n_head, tokens), out_shap...]
where the time goes in v3:
time: 57.3 us; the launch traced here: 57.1 us
  Pallas kernels  54.8 us (96%)
  local copies, waits for them, and re-layouts  2.29 us (4%)
    pallas_call x1, Pallas kernels, on_device(): pl.pallas_call(functools.partial(kernel, n_seq, n_head, tokens), out_shap...  54.8 us
    unnamed x1, local copies, waits for them, and re-layouts  2.29 us

profile of v3, /device:TPU:29, one launch (start us, length us, event | category | flops | bytes accessed | tf_op | source)
XLA Modules:
  0.0 57.1 jit_solution(17460072931667691572)
XLA Ops:
  0.0 54.8 %shard_map.46 = bf16[128,4096]{1,0:T(8,128)(2,1)} custom-call(bf16[128,4096]{1,0:T(8,128)(2,1)} %q_hbm.1, bf16[128,4096]{1,0:T(8,128)(2,1)} %k_hbm.1, bf16[128,4096]{1,0:T(8,128)(2,1)} %v_hbm.1, s32[8]{0:T(128)} %doc_ref.1), custom_call_target="tpu_custom_call" | custom-call | flops 1073741824 | bytes 4194304 | tf_op jit(solution)/shard_map/pallas_call | solution.py:275
  54.8 2.3 %copy.6 = bf16[128,4096]{1,0:T(8,128)(2,1)} copy(bf16[128,4096]{1,0:T(8,128)(2,1)} %shard_map.46) | data formatting | bytes 2097152

commit v4 on v3

--- a/solution.py
+++ b/solution.py
@@ -71,8 +71,7 @@
             copy.wait() if r == 0 else copy.wait_recv()
 
     groups = [("kv", chunk) for chunk in range(chunks)]
-    groups.insert(max(chunks - 1, 2), ("q", 0))
-    groups += [("q", chunk) for chunk in range(1, chunks)]
+    groups += [("q", chunk) for chunk in range(chunks)]
 
     def send_group(index):
         if index < len(groups):
@@ -230,18 +229,22 @@
         final[chunk] = max(final[chunk], groups.index(("q", chunk)))
     for index, (kind, chunk) in enumerate(groups):
         wait_group(index)
-        if kind == "kv":
-            increment(chunk)
-            pair_copy(chunk).start()
-        else:
-            soft_part(chunk)
-        for other in range(chunks):
-            if ready[other] <= index <= final[other]:
-                turn = index - ready[other]
-
-                @pl.when(z >= turn if index == final[other] else z == turn)
-                def _():
-                    forward(other)
+        for step in ("middle", "work", "end"):
+            if step == "work":
+                if kind == "kv":
+                    increment(chunk)
+                    pair_copy(chunk).start()
+                else:
+                    soft_part(chunk)
+                continue
+            for other in range(chunks):
+                ends = index == final[other]
+                if ready[other] <= index <= final[other] and ends == (step == "end"):
+                    turn = index - ready[other]
+
+                    @pl.when(z >= turn if ends else z == turn)
+                    def _():
+                        forward(other)
 
         for other in range(chunks):
             if final[other] == index:

time: 57.3 us -> 59.1 us (1.031)
  the two profiles are of different devices: /device:TPU:29 before, /device:TPU:0 now
where the time goes in v4:
time: 59.1 us; the launch traced here: 58.9 us
  Pallas kernels  56.6 us (96%)
  local copies, waits for them, and re-layouts  2.29 us (4%)
    pallas_call x1, Pallas kernels, on_device(): pl.pallas_call(functools.partial(kernel, n_seq, n_head, tokens), out_shap...  56.6 us
    unnamed x1, local copies, waits for them, and re-layouts  2.29 us

profile of v4, /device:TPU:0, one launch (start us, length us, event | category | flops | bytes accessed | tf_op | source)
XLA Modules:
  0.0 58.9 jit_solution(13648645029681712176)
XLA Ops:
  0.0 56.6 %shard_map.46 = bf16[128,4096]{1,0:T(8,128)(2,1)} custom-call(bf16[128,4096]{1,0:T(8,128)(2,1)} %q_hbm.1, bf16[128,4096]{1,0:T(8,128)(2,1)} %k_hbm.1, bf16[128,4096]{1,0:T(8,128)(2,1)} %v_hbm.1, s32[8]{0:T(128)} %doc_ref.1), custom_call_target="tpu_custom_call" | custom-call | flops 1073741824 | bytes 4194304 | tf_op jit(solution)/shard_map/pallas_call | solution.py:278
  56.7 2.3 %copy.6 = bf16[128,4096]{1,0:T(8,128)(2,1)} copy(bf16[128,4096]{1,0:T(8,128)(2,1)} %shard_map.46) | data formatting | bytes 2097152

commit v5 on v4

--- a/solution.py
+++ b/solution.py
@@ -71,7 +71,8 @@
             copy.wait() if r == 0 else copy.wait_recv()
 
     groups = [("kv", chunk) for chunk in range(chunks)]
-    groups += [("q", chunk) for chunk in range(chunks)]
+    groups.insert(max(chunks - 1, 2), ("q", 0))
+    groups += [("q", chunk) for chunk in range(1, chunks)]
 
     def send_group(index):
         if index < len(groups):
@@ -239,7 +240,7 @@
                 continue
             for other in range(chunks):
                 ends = index == final[other]
-                if ready[other] <= index <= final[other] and ends == (step == "end"):
+                if ready[other] <= index <= final[other] and (ends or kind == "kv") == (step == "end"):
                     turn = index - ready[other]
 
                     @pl.when(z >= turn if ends else z == turn)

time: 59.1 us -> 60.3 us (1.020)
  the two profiles are of different devices: /device:TPU:0 before, /device:TPU:29 now
where the time goes in v5:
time: 60.3 us; the launch traced here: 60.1 us
  Pallas kernels  57.8 us (96%)
  local copies, waits for them, and re-layouts  2.29 us (4%)
    pallas_call x1, Pallas kernels, on_device(): pl.pallas_call(functools.partial(kernel, n_seq, n_head, tokens), out_shap...  57.8 us
    unnamed x1, local copies, waits for them, and re-layouts  2.29 us

profile of v5, /device:TPU:29, one launch (start us, length us, event | category | flops | bytes accessed | tf_op | source)
XLA Modules:
  0.0 60.1 jit_solution(17311523526514896131)
XLA Ops:
  0.0 57.8 %shard_map.46 = bf16[128,4096]{1,0:T(8,128)(2,1)} custom-call(bf16[128,4096]{1,0:T(8,128)(2,1)} %q_hbm.1, bf16[128,4096]{1,0:T(8,128)(2,1)} %k_hbm.1, bf16[128,4096]{1,0:T(8,128)(2,1)} %v_hbm.1, s32[8]{0:T(128)} %doc_ref.1), custom_call_target="tpu_custom_call" | custom-call | flops 1073741824 | bytes 4194304 | tf_op jit(solution)/shard_map/pallas_call | solution.py:279
  57.8 2.3 %copy.6 = bf16[128,4096]{1,0:T(8,128)(2,1)} copy(bf16[128,4096]{1,0:T(8,128)(2,1)} %shard_map.46) | data formatting | bytes 2097152
